TPU v7x, 32 devices: a whole 2x2x4 slice. The times are simulated.
32 devices in a mesh: ctx: 8 (over z, y), ulysses: 4 (over x, core).
Axes of the slice: x: 2, y: 2, z: 4, core: 2. Of those that a mesh axis runs over, the one named last changes fastest.
Arguments:
- queries: bfloat16 [4096, 6144], P(('ctx', 'ulysses')), may hold values from -120 to 120
- keys: bfloat16 [4096, 1024], P(('ctx', 'ulysses')), may hold values from -4 to 4
- values: bfloat16 [4096, 1024], P(('ctx', 'ulysses')), may hold values from -6 to 6
- doc_ids: int32 [4096], replicated, may hold values from 0 to 47, never falling along the last dimension, each value on 1 to 128 neighbouring positions
Outputs:
- attended: bfloat16 [4096, 6144], P(('ctx', 'ulysses'))
Inputs may be any that keep to these rules, and one draw needn't show every extreme that they name: `doc_ids`: document numbers never fall along the tokens; every document holds at most 128 tokens and one holds exactly that many.
All inputs are finite; a program needn't handle non-finite values.
Results may differ from a plain program's by a relative error of at most 0.001.
Values may be sent and summed in bfloat16 or wider, within the bound.
No kernel may reach another device: no remote copies, remote signals or barrier semaphores. Data moves between devices by JAX's collectives and lax.ppermute only.
A program may use at most 64 MiB of HBM per device.

v0:
```python
import math

import jax
import jax.numpy as jnp
from jax import lax
from jax.sharding import PartitionSpec as P

HQ = 48
KV = 8
HEAD = 128


def from_behind(value, axis, steps):
    count = lax.axis_size(axis)
    leading, last = (max(0, -steps), min(count, count - steps))
    return lax.ppermute(value, axis, [(source, source + steps) for source in range(leading, last)])


def tile_length():
    return 512


def pack_heads(key_rows, value_rows, groups):
    local_tokens = key_rows.shape[0]
    if KV % groups == 0:
        kv_slots = KV // groups
        key_send = key_rows.reshape(local_tokens, groups, kv_slots * HEAD)
        value_send = value_rows.reshape(local_tokens, groups, kv_slots * HEAD)
    else:
        copies = groups // KV
        key_send = jnp.repeat(key_rows.reshape(local_tokens, KV, HEAD), copies, axis=1)
        value_send = jnp.repeat(value_rows.reshape(local_tokens, KV, HEAD), copies, axis=1)
    return jnp.concatenate([key_send, value_send], axis=2).reshape(local_tokens, -1)


def shards(queries, keys, values, doc_ids):
    groups = lax.axis_size("ulysses")
    local_tokens = queries.shape[0]
    block_len = groups * local_tokens
    reach = block_len // 4
    query_slots = HQ // groups
    kv_slots = KV // groups if KV % groups == 0 else 1
    per_kv = query_slots // kv_slots
    kv_width = kv_slots * HEAD
    query_recv = lax.all_to_all(queries, "ulysses", split_axis=1, concat_axis=0, tiled=True)
    kv_block = lax.all_to_all(
        pack_heads(keys, values, groups), "ulysses", split_axis=1, concat_axis=0, tiled=True
    )
    query_rows = query_recv.reshape(block_len, kv_slots, per_kv, HEAD).transpose(1, 2, 0, 3)
    own_first = lax.axis_index("ctx") * block_len
    tail_rows = from_behind(kv_block[block_len - reach :], "ctx", 1)
    combined = jnp.concatenate([tail_rows, kv_block], axis=0)
    key_all = combined[:, :kv_width].reshape(-1, kv_slots, HEAD)
    value_all = combined[:, kv_width:].reshape(-1, kv_slots, HEAD)
    doc_pad = jnp.concatenate([jnp.full((reach,), -1, jnp.int32), doc_ids], axis=0)
    key_doc_all = lax.dynamic_slice_in_dim(doc_pad, own_first, reach + block_len, 0)
    query_doc = key_doc_all[reach:]
    query_len = tile_length()
    scale_factor = 1.0 / math.sqrt(HEAD)
    finished = []
    for query_start in range(0, block_len, query_len):
        tile_rows = query_rows[:, :, query_start : query_start + query_len]
        query_pos = own_first + query_start + jnp.arange(query_len, dtype=jnp.int32)
        tile_doc = query_doc[query_start : query_start + query_len]
        key_tile = key_all[query_start : query_start + reach + query_len]
        value_tile = value_all[query_start : query_start + reach + query_len]
        key_doc = key_doc_all[query_start : query_start + reach + query_len]
        key_pos = own_first - reach + query_start + jnp.arange(reach + query_len, dtype=jnp.int32)
        visible = (
            (key_doc[None, :] == tile_doc[:, None])
            & (key_pos[None, :] <= query_pos[:, None])
            & (key_pos[None, :] >= 0)
        )
        scores = (
            jnp.einsum("sgrd,ksd->sgrk", tile_rows, key_tile, preferred_element_type=jnp.float32)
            * scale_factor
        )
        masked = jnp.where(visible[None, None], scores, -1e30)
        peak = jnp.max(masked, axis=-1, keepdims=True)
        weights = jnp.where(visible[None, None], jnp.exp(scores - peak), 0.0)
        totals = jnp.sum(weights, axis=-1)
        mixed = jnp.einsum(
            "sgrk,ksd->sgrd",
            weights.astype(jnp.bfloat16),
            value_tile,
            preferred_element_type=jnp.float32,
        )
        finished.append((mixed / totals[..., None]).astype(jnp.bfloat16))
    output = jnp.concatenate(finished, axis=2)
    output = output.transpose(2, 0, 1, 3).reshape(block_len, query_slots * HEAD)
    return lax.all_to_all(output, "ulysses", split_axis=0, concat_axis=1, tiled=True)


def solution(mesh):
    placed = (
        P(("ctx", "ulysses"), None),
        P(("ctx", "ulysses"), None),
        P(("ctx", "ulysses"), None),
        P(),
    )
    return jax.shard_map(
        shards, mesh=mesh, in_specs=placed, out_specs=P(("ctx", "ulysses"), None), check_vma=False
    )
```

profile of v0, /device:TPU:16, one launch (start us, length us, event | category | flops | bytes accessed | tf_op | source)
XLA Modules:
  0.0 90.2 jit_solution(17291032318856919589)
XLA Ops:
  0.0 0.0 copy-start
  0.0 1.2 %copy.28 = bf16[128,1024]{0,1:T(8,128)(2,1)S(1)} copy(bf16[128,1024]{1,0:T(8,128)(2,1)} %param.5) | data formatting | bytes 524288 | tf_op args[1]
  1.2 1.1 %copy.29 = bf16[128,1024]{0,1:T(8,128)(2,1)S(1)} copy(bf16[128,1024]{1,0:T(8,128)(2,1)} %param.6) | data formatting | bytes 524288 | tf_op args[2]
  2.4 0.8 pad_maximum_fusion
  3.2 3.5 %all-to-all-start = ((bf16[128,4,512]{0,2,1:T(8,128)(2,1)}), bf16[128,4,512]{0,2,1:T(8,128)(2,1)S(1)}, u32[]{:S(2)}, u32[]{:S(2)}) async-start(bf16[128,4,512]{0,2,1:T(8,128)(2,1)} %pad_maximum_fusion), calls=%async_computation | async-start | bytes 1048576 | tf_op jit(solution)/shard_map/all_to_all | solution.py:46
  6.7 0.0 copy-done
  6.7 0.0 copy-start.2
  6.7 1.6 %copy.33 = bf16[128,6144]{0,1:T(8,128)(2,1)} copy(bf16[128,6144]{1,0:T(8,128)(2,1)S(1)} %copy-done) | data formatting | bytes 3145728 | tf_op args[0]
  8.3 7.2 %all-to-all-done = bf16[128,4,512]{0,2,1:T(8,128)(2,1)S(1)} async-done(((bf16[128,4,512]{0,2,1:T(8,128)(2,1)}), bf16[128,4,512]{0,2,1:T(8,128)(2,1)S(1)}, u32[]{:S(2)}, u32[]{:S(2)}) %all-to-all-start) | async-done | bytes 524320 | tf_op jit(solution)/shard_map/all_to_all | solution.py:46
  15.5 3.6 %all-to-all-start.1 = ((bf16[128,4,1536]{0,2,1:T(8,128)(2,1)}), bf16[128,4,1536]{0,2,1:T(8,128)(2,1)S(1)}, u32[]{:S(2)}, u32[]{:S(2)}) async-start(bf16[128,4,1536]{0,2,1:T(8,128)(2,1)} %bitcast.7), calls=%async_computation.1 | async-start | bytes 3145728 | tf_op jit(solution)/shard_map/all_to_all | solution.py:45
  19.1 0.0 copy-done.2
  19.1 0.1 pad_dynamic-slice_fusion
  19.2 0.1 copy.30
  19.3 3.4 %collective-permute-start = (bf16[128,512]{1,0:T(8,128)(2,1)S(1)}, bf16[128,512]{1,0:T(8,128)(2,1)S(1)}, u32[]{:S(2)}, u32[]{:S(2)}) collective-permute-start(bf16[128,512]{1,0:T(8,128)(2,1)S(1)} %bitcast.71), channel_id=1, source_target_pairs={{0,4},{4,8},{8,12},{12,16},{16,20},{20,24},{24,28},{1,5},{5,9},{9,... | collective-permute-start | bytes 393224 | tf_op jit(solution)/shard_map/ppermute | solution.py:16
  22.8 0.4 and_and_fusion
  23.1 0.2 copy.31
  23.4 4.6 %collective-permute-done = bf16[128,512]{1,0:T(8,128)(2,1)S(1)} collective-permute-done((bf16[128,512]{1,0:T(8,128)(2,1)S(1)}, bf16[128,512]{1,0:T(8,128)(2,1)S(1)}, u32[]{:S(2)}, u32[]{:S(2)}) %collective-permute-start) | collective-permute-done | bytes 131104 | tf_op jit(solution)/shard_map/ppermute | solution.py:16
  28.0 0.9 %copy.32 = bf16[640,256]{0,1:T(8,128)(2,1)} copy(bf16[640,256]{1,0:T(8,128)(2,1)S(1)} %get-tuple-element.5) | data formatting | bytes 655360 | tf_op jit(solution)/shard_map/slice | solution.py:53
  29.0 0.9 copy.37
  29.8 9.3 %all-to-all-done.1 = bf16[128,4,1536]{0,2,1:T(8,128)(2,1)S(1)} async-done(((bf16[128,4,1536]{0,2,1:T(8,128)(2,1)}), bf16[128,4,1536]{0,2,1:T(8,128)(2,1)S(1)}, u32[]{:S(2)}, u32[]{:S(2)}) %all-to-all-start.1) | async-done | bytes 1572896 | tf_op jit(solution)/shard_map/all_to_all | solution.py:45
  39.1 7.3 %copy.34 = bf16[4,128,1536]{1,0,2:T(4,128)(2,1)S(1)} copy(bf16[4,128,1536]{1,2,0:T(8,128)(2,1)S(1)} %bitcast.62) | data formatting | bytes 3145728 | tf_op jit(solution)/shard_map/all_to_all | solution.py:45
  46.4 0.6 reshape.117
  47.1 0.9 copy.35
  48.0 0.0 copy-start.1
  48.0 10.4 %fusion.25 = (f32[2,6,512]{2,1,0:T(8,128)S(1)}, bf16[2,6,512,640]{2,3,1,0:T(8,128)(2,1)}) fusion(pred[512,640]{0,1:T(8,128)(4,1)S(1)} %and_and_fusion, bf16[640,2,128,1]{0,2,3,1:T(8,128)(2,1)} %bitcast.70, bf16[512,2,6,128]{3,0,2,1:T(8,128)(2,1)S(1)} %copy.35), kind=kOutput, calls=%fused_computation.30 | convolution fusion | flops 2040791680 | bytes 10117120 | tf_op jit(solution)/shard_map/sub | solution.py:80
  58.4 0.0 copy-done.1
  58.4 6.3 %fusion.10 = bf16[512,2,6,128]{3,0,2,1:T(8,128)(2,1)S(1)} fusion(bf16[640,2,128,1]{0,2,3,1:T(8,128)(2,1)S(1)} %bitcast.69, bf16[2,6,512,640]{2,3,1,0:T(8,128)(2,1)} %get-tuple-element.8, f32[512,2,6]{0,2,1:T(8,128)S(1)} %bitcast.72), kind=kOutput, calls=%fused_computation.13 | convolution fusion | flops 1008205824 | bytes 9789440 | tf_op jit(solution)/shard_map/sgrk,ksd->sgrd/dot_general | solution.py:82
  64.7 0.7 copy.40
  65.4 0.4 all_to_all.44
  65.9 0.2 copy.41
  66.1 22.5 %all_to_all.51 = bf16[4,128,1536]{1,2,0:T(8,128)(2,1)S(1)} all-to-all(bf16[4,128,1536]{1,2,0:T(8,128)(2,1)S(1)} %copy.41), channel_id=1, replica_groups=mesh['ctx'=8,'ulysses'=4] {'ulysses'}, dimensions={0} | all-to-all | bytes 3145728 | tf_op jit(solution)/shard_map/all_to_all | solution.py:91
  88.6 1.6 %copy.42 = bf16[128,6144]{1,0:T(8,128)(2,1)} copy(bf16[128,6144]{0,1:T(8,128)(2,1)S(1)} %bitcast.63) | data formatting | bytes 3145728 | tf_op jit(solution)/shard_map/all_to_all | solution.py:91
  (5 shorter events, 0.1 us)
Async XLA Ops:
  0.0 6.7 %copy-start = (bf16[128,6144]{1,0:T(8,128)(2,1)S(1)}, bf16[128,6144]{1,0:T(8,128)(2,1)}, u32[]{:S(2)}) copy-start(bf16[128,6144]{1,0:T(8,128)(2,1)} %param.4) | copy-start | bytes 4718596
  3.2 12.3 %all-to-all-start = ((bf16[128,4,512]{0,2,1:T(8,128)(2,1)}), bf16[128,4,512]{0,2,1:T(8,128)(2,1)S(1)}, u32[]{:S(2)}, u32[]{:S(2)}) async-start(bf16[128,4,512]{0,2,1:T(8,128)(2,1)} %pad_maximum_fusion), calls=%async_computation | async-start | bytes 1048576 | tf_op jit(solution)/shard_map/all_to_all | solution.py:46
  6.7 12.4 %copy-start.2 = (s32[4096]{0:T(1024)S(1)}, s32[4096]{0:T(1024)}, u32[]{:S(2)}) copy-start(s32[4096]{0:T(1024)} %param.7) | copy-start | bytes 49156
  15.5 23.6 %all-to-all-start.1 = ((bf16[128,4,1536]{0,2,1:T(8,128)(2,1)}), bf16[128,4,1536]{0,2,1:T(8,128)(2,1)S(1)}, u32[]{:S(2)}, u32[]{:S(2)}) async-start(bf16[128,4,1536]{0,2,1:T(8,128)(2,1)} %bitcast.7), calls=%async_computation.1 | async-start | bytes 3145728 | tf_op jit(solution)/shard_map/all_to_all | solution.py:45
  19.3 8.6 %collective-permute-start = (bf16[128,512]{1,0:T(8,128)(2,1)S(1)}, bf16[128,512]{1,0:T(8,128)(2,1)S(1)}, u32[]{:S(2)}, u32[]{:S(2)}) collective-permute-start(bf16[128,512]{1,0:T(8,128)(2,1)S(1)} %bitcast.71), channel_id=1, source_target_pairs={{0,4},{4,8},{8,12},{12,16},{16,20},{20,24},{24,28},{1,5},{5,9},{9,... | collective-permute-start | bytes 393224 | tf_op jit(solution)/shard_map/ppermute | solution.py:16
  48.0 10.5 %copy-start.1 = (bf16[640,256]{0,1:T(8,128)(2,1)S(1)}, bf16[640,256]{0,1:T(8,128)(2,1)}, u32[]{:S(2)}) copy-start(bf16[640,256]{0,1:T(8,128)(2,1)} %copy.37) | copy-start | bytes 983044
where the time goes:
time: 91.3 us; the launch traced here: 90.2 us
  blocking collectives  22.5 us (25%)
  waiting for transfers between devices  21.1 us (23%)
  local copies, waits for them, and re-layouts  17.9 us (20%)
  matrix products  16.7 us (18%)
  starting transfers between devices  10.5 us (12%)
  other arithmetic  1.33 us (1%)
    all_to_all x1, blocking collectives, shards(): lax.all_to_all(output, 'ulysses', split_axis=0, concat_axis=1, tiled=True)  22.5 us
    sub x1, matrix products, shards(): weights = jnp.where(visible[None, None], jnp.exp(scores - peak), 0.0)  10.4 us
    all_to_all x1, waiting for transfers between devices, shards(): lax.all_to_all(queries, 'ulysses', split_axis=1, concat_axis=0, tiled=True)  9.26 us
    all_to_all x1, local copies, waits for them, and re-layouts, shards(): lax.all_to_all(queries, 'ulysses', split_axis=1, concat_axis=0, tiled=True)  7.3 us
    all_to_all x1, waiting for transfers between devices, shards(): lax.all_to_all(pack_heads(keys, values, groups), 'ulysses', split_axis=1,...  7.22 us
    dot_general x1, matrix products, shards(): jnp.einsum('sgrk,ksd->sgrd', weights.astype(jnp.bfloat16), value_tile, pr...  6.27 us
    ppermute x1, waiting for transfers between devices, from_behind(): lax.ppermute(value, axis, [(source, source + steps) for source in range(l...  4.61 us
    unnamed x9, local copies, waits for them, and re-layouts  3.94 us
  transfers between devices with their start and end apart: 3, of which 3 were waited for; matrix products, arithmetic and copies ran while one was open for 5% of the time, Pallas kernels for 0%

commit v1 on v0

v1 whole, which is shorter than its diff:
```python
import functools
import math

import jax
import jax.numpy as jnp
from jax import lax
from jax.experimental import pallas as pl
from jax.experimental.pallas import tpu as pltpu
from jax.sharding import PartitionSpec as P

HQ = 48
KV = 8
HEAD = 128
PER_KV = HQ // KV
TOKENS_AXES = ("ctx", "ulysses")
HIDDEN = -1e30
EXPONENT = math.log2(math.e) / math.sqrt(HEAD)
KERNEL_VMEM = 16 * 1024 * 1024


def two_rings(count, cut):
    first = [(i, i + 1) for i in range(cut)] + [(cut, 0)]
    second = [(i, i + 1) for i in range(cut + 1, count - 1)] + [(count - 1, cut + 1)]
    return first + second


def ring(count, steps):
    return [(i, (i + steps) % count) for i in range(count)]


def swapped(count):
    return [(i, i ^ 1) for i in range(count)]


def head_columns(head):
    return pl.ds(pl.multiple_of(head * HEAD, HEAD), HEAD)


def softmax_parts(raw):
    peak = jnp.max(raw, axis=1, keepdims=True)
    weights = jnp.exp2((raw - peak) * EXPONENT)
    totals = jnp.sum(weights, axis=1, keepdims=True)
    return weights.astype(jnp.bfloat16), 1.0 / totals


def own_kernel(query, key, value, docs, early, own, cross_bias, crossing, own_bias, sems):
    length = key.shape[0]
    me = lax.axis_index(TOKENS_AXES)
    own_docs = docs[pl.ds(me, 1), :]
    before = docs[pl.ds(jnp.maximum(me - 1, 0), 1), :]
    before = jnp.where(me > 0, before, -1)
    row = lax.broadcasted_iota(jnp.int32, (length, length), 0)
    column = lax.broadcasted_iota(jnp.int32, (length, length), 1)
    row_doc = jnp.sum(jnp.where(row == column, own_docs, 0), axis=1, keepdims=True)
    own_seen = (row_doc == own_docs) & (column <= row)
    before_seen = row_doc == before
    own_bias[...] = jnp.where(own_seen, 0.0, HIDDEN)
    cross_bias[...] = jnp.where(own_seen | before_seen, 0.0, HIDDEN)
    from_before = row_doc == before[:, length - 1 :]
    crossing[...] = jnp.where(jnp.broadcast_to(from_before, (length, length)), 1.0, 0.0).astype(jnp.bfloat16)

    def group(g, carry):
        keys = key[:, head_columns(g)]
        values = value[:, head_columns(g)]
        for j in range(PER_KV):
            columns = head_columns(g * PER_KV + j)
            raw = lax.dot_general(
                query[:, columns], keys, (((1,), (1,)), ((), ())), preferred_element_type=jnp.float32
            )
            weights, share = softmax_parts(raw + own_bias[...])
            mixed = jnp.dot(weights, values, preferred_element_type=jnp.float32)
            own[:, columns] = (mixed * share).astype(jnp.bfloat16)
        return carry

    lax.fori_loop(0, KV, group, 0)


def weight_kernel(query, key, key_far, key_near, cross_bias, crossing, weights_out, share_out, *, cut):
    from_near = lax.axis_index(TOKENS_AXES) == cut + 1
    mine = crossing[...] > 0

    def group(g, carry):
        columns = head_columns(g)
        behind = jnp.where(from_near, key_near[:, columns], key_far[:, columns])
        keys = jnp.where(mine, key[:, columns], behind)
        for j in range(PER_KV):
            raw = lax.dot_general(
                query[:, head_columns(g * PER_KV + j)], keys, (((1,), (1,)), ((), ())), preferred_element_type=jnp.float32
            )
            weights, share = softmax_parts(raw + cross_bias[...])
            weights_out[g * PER_KV + j] = weights
            share_out[g * PER_KV + j] = jnp.broadcast_to(share, share_out.shape[1:])
        return carry

    lax.fori_loop(0, KV, group, 0)


def merge_kernel(weights, share, value, value_far, value_near, crossing, own, out, held, sems, *, cut):
    from_near = lax.axis_index(TOKENS_AXES) == cut + 1
    mine = crossing[...] > 0
    width = PER_KV * HEAD

    def copy(g):
        columns = pl.ds(g * width, width)
        return pltpu.make_async_copy(held.at[:, columns], out.at[:, columns], sems.at[g])

    for g in range(KV):
        columns = slice(g * HEAD, (g + 1) * HEAD)
        behind = jnp.where(from_near, value_near[:, columns], value_far[:, columns])
        values = jnp.where(mine, value[:, columns], behind)
        for j in range(PER_KV):
            head = g * PER_KV + j
            mixed = jnp.dot(weights[head], values, preferred_element_type=jnp.float32)
            fresh = (mixed * share[head]).astype(jnp.bfloat16)
            held[:, head * HEAD : (head + 1) * HEAD] = jnp.where(mine, fresh, own[:, head * HEAD : (head + 1) * HEAD])
        copy(g).start()
    for g in range(KV):
        copy(g).wait()


def in_vmem(array):
    return pltpu.with_memory_space_constraint(array, pltpu.VMEM)


def one_block_back(queries, keys, values, doc_ids):
    count = lax.axis_size(TOKENS_AXES)
    length = queries.shape[0]
    cut = count // 2 - 2
    rings, swap = two_rings(count, cut), swapped(count)
    key_near = lax.ppermute(keys, TOKENS_AXES, swap)
    key_far = lax.ppermute(keys, TOKENS_AXES, rings)
    value_near = lax.ppermute(values, TOKENS_AXES, swap)
    value_far = lax.ppermute(values, TOKENS_AXES, rings)
    docs = doc_ids.reshape(-1, length)
    whole = pl.BlockSpec(memory_space=pltpu.VMEM)
    params = pltpu.CompilerParams(vmem_limit_bytes=KERNEL_VMEM)
    square = (length, length)
    queries = in_vmem(queries)
    own, cross_bias, crossing = pl.pallas_call(
        lambda q, k, v, d, o, b, c, ob: own_kernel(q, k, v, d, None, o, b, c, ob, None),
        out_shape=(
            pltpu.VMEM(queries.shape, jnp.bfloat16),
            pltpu.VMEM(square, jnp.float32),
            pltpu.VMEM(square, jnp.bfloat16),
        ),
        in_specs=[whole] * 4,
        out_specs=[whole] * 3,
        scratch_shapes=[pltpu.VMEM(square, jnp.float32)],
        compiler_params=params,
        name="own_attention",
    )(queries, in_vmem(keys), in_vmem(values), in_vmem(docs))
    weights, share = pl.pallas_call(
        functools.partial(weight_kernel, cut=cut),
        out_shape=(
            pltpu.VMEM((HQ,) + square, jnp.bfloat16),
            pltpu.VMEM((HQ,) + square, jnp.float32),
        ),
        in_specs=[whole] * 6,
        out_specs=[whole] * 2,
        compiler_params=params,
        name="crossing_weights",
    )(queries, in_vmem(keys), in_vmem(key_far), in_vmem(key_near), cross_bias, crossing)
    return pl.pallas_call(
        functools.partial(merge_kernel, cut=cut),
        out_shape=jax.ShapeDtypeStruct(queries.shape, jnp.bfloat16),
        in_specs=[whole] * 7,
        out_specs=pl.BlockSpec(memory_space=pl.ANY),
        scratch_shapes=[pltpu.VMEM(queries.shape, jnp.bfloat16), pltpu.SemaphoreType.DMA((KV,))],
        compiler_params=params,
        name="merge",
    )(weights, share, in_vmem(values), in_vmem(value_far), in_vmem(value_near), crossing, own)


def blocks_back(queries, keys, values, doc_ids, blocks):
    count = lax.axis_size(TOKENS_AXES)
    length = queries.shape[0]
    me = lax.axis_index(TOKENS_AXES)
    halo = [
        (lax.ppermute(keys, TOKENS_AXES, ring(count, s)), lax.ppermute(values, TOKENS_AXES, ring(count, s)))
        for s in range(blocks, 0, -1)
    ] + [(keys, values)]
    window = (blocks + 1) * length
    key_all = jnp.concatenate([k for k, _ in halo], axis=0).reshape(window, KV, HEAD).transpose(1, 0, 2)
    value_all = jnp.concatenate([v for _, v in halo], axis=0).reshape(window, KV, HEAD).transpose(1, 0, 2)
    padded = jnp.concatenate([jnp.full((blocks * length,), -1, jnp.int32), doc_ids], axis=0)
    key_doc = lax.dynamic_slice_in_dim(padded, me * length, window, 0)
    query_doc = key_doc[blocks * length :]
    offset = jnp.arange(window, dtype=jnp.int32) - blocks * length
    visible = (key_doc[None, :] == query_doc[:, None]) & (offset[None, :] <= jnp.arange(length)[:, None])
    grouped = queries.reshape(length, KV, PER_KV, HEAD).transpose(1, 2, 0, 3)

    def one_head(operands):
        rows, key_rows, value_rows = operands
        raw = jnp.einsum("gqd,kd->gqk", rows, key_rows, preferred_element_type=jnp.float32)
        raw = jnp.where(visible[None], raw, HIDDEN)
        peak = jnp.max(raw, axis=-1, keepdims=True)
        weights = jnp.exp2((raw - peak) * EXPONENT)
        totals = jnp.sum(weights, axis=-1, keepdims=True)
        mixed = jnp.einsum("gqk,kd->gqd", weights.astype(jnp.bfloat16), value_rows, preferred_element_type=jnp.float32)
        return (mixed / totals).astype(jnp.bfloat16)

    mixed = lax.map(one_head, (grouped, key_all, value_all))
    return mixed.transpose(2, 0, 1, 3).reshape(length, HQ * HEAD)


def shards(queries, keys, values, doc_ids):
    length = queries.shape[0]
    reach = lax.axis_size("ulysses") * length // 4
    blocks = -(-reach // length)
    if blocks == 1 and length == HEAD:
        return one_block_back(queries, keys, values, doc_ids)
    return blocks_back(queries, keys, values, doc_ids, blocks)


def solution(mesh):
    placed = P(TOKENS_AXES, None)
    return jax.shard_map(
        shards, mesh=mesh, in_specs=(placed, placed, placed, P()), out_specs=placed, check_vma=False
    )
```

time: 91.3 us -> 25.7 us (0.28)
  the two profiles are of different devices: /device:TPU:16 before, /device:TPU:0 now
where the time goes in v1:
time: 25.7 us; the launch traced here: 25.4 us
  Pallas kernels  17.8 us (69%)
  local copies, waits for them, and re-layouts  4.03 us (16%)
  starting transfers between devices  3.56 us (14%)
    pallas_call x1, Pallas kernels, one_block_back(): pl.pallas_call(lambda q, k, v, d, o, b, c, ob: own_kernel(q, k, v, d, Non...  12.6 us
    unnamed x10, local copies, waits for them, and re-layouts  4.03 us
    pallas_call x1, Pallas kernels, one_block_back(): pl.pallas_call(functools.partial(weight_kernel, cut=cut), out_shape=(pltp...  3.65 us
    ppermute x1, starting transfers between devices, one_block_back(): value_far = lax.ppermute(values, TOKENS_AXES, rings)  2.55 us
    pallas_call x1, Pallas kernels, one_block_back(): pl.pallas_call(functools.partial(merge_kernel, cut=cut), out_shape=jax.Sh...  1.48 us
  transfers between devices with their start and end apart: 4, of which 0 were waited for; matrix products, arithmetic and copies ran while one was open for 0% of the time, Pallas kernels for 64%

profile of v1, /device:TPU:0, one launch (start us, length us, event | category | flops | bytes accessed | tf_op | source)
XLA Modules:
  0.0 25.4 jit_solution(7043209375889953673)
XLA Ops:
  0.0 0.5 %collective-permute-start.1 = (bf16[128,1024]{1,0:T(8,128)(2,1)}, bf16[128,1024]{1,0:T(8,128)(2,1)S(1)}, u32[]{:S(2)}, u32[]{:S(2)}) collective-permute-start(bf16[128,1024]{1,0:T(8,128)(2,1)} %key.1), channel_id=1, source_target_pairs={{0,1},{1,0},{2,3},{3,2},{4,5},{5,4},{6,7},{7,6},{8,9},{9,8},{10,11... | collective-permute-start | bytes 786440 | tf_op jit(solution)/shard_map/ppermute | solution.py:130
  0.5 0.1 collective-permute-start
  0.5 2.5 %collective-permute-start.2 = (bf16[128,1024]{1,0:T(8,128)(2,1)}, bf16[128,1024]{1,0:T(8,128)(2,1)S(1)}, u32[]{:S(2)}, u32[]{:S(2)}) collective-permute-start(bf16[128,1024]{1,0:T(8,128)(2,1)} %value.1), channel_id=1, source_target_pairs={{0,1},{1,2},{2,3},{3,4},{4,5},{5,6},{6,7},{7,8},{8,9},{9,10},{10,1... | collective-permute-start | bytes 786440 | tf_op jit(solution)/shard_map/ppermute | solution.py:133
  3.1 0.5 %collective-permute-start.3 = (bf16[128,1024]{1,0:T(8,128)(2,1)}, bf16[128,1024]{1,0:T(8,128)(2,1)S(1)}, u32[]{:S(2)}, u32[]{:S(2)}) collective-permute-start(bf16[128,1024]{1,0:T(8,128)(2,1)} %value.1), channel_id=1, source_target_pairs={{0,1},{1,0},{2,3},{3,2},{4,5},{5,4},{6,7},{7,6},{8,9},{9,8},{10,11... | collective-permute-start | bytes 786440 | tf_op jit(solution)/shard_map/ppermute | solution.py:132
  3.6 0.0 copy-start
  3.6 1.4 %copy-done = bf16[128,6144]{1,0:T(8,128)(2,1)S(1)} copy-done((bf16[128,6144]{1,0:T(8,128)(2,1)S(1)}, bf16[128,6144]{1,0:T(8,128)(2,1)}, u32[]{:S(2)}) %copy-start) | copy-done | bytes 1572888
  5.0 0.0 copy-start.1
  5.0 0.9 %copy-done.1 = bf16[128,1024]{1,0:T(8,128)(2,1)S(1)} copy-done((bf16[128,1024]{1,0:T(8,128)(2,1)S(1)}, bf16[128,1024]{1,0:T(8,128)(2,1)}, u32[]{:S(2)}) %copy-start.1) | copy-done | bytes 262168
  5.9 0.0 copy-start.2
  5.9 0.9 %copy-done.2 = bf16[128,1024]{1,0:T(8,128)(2,1)S(1)} copy-done((bf16[128,1024]{1,0:T(8,128)(2,1)S(1)}, bf16[128,1024]{1,0:T(8,128)(2,1)}, u32[]{:S(2)}) %copy-start.2) | copy-done | bytes 262168
  6.9 0.0 copy-start.4
  6.9 0.7 %copy-done.4 = s32[4096]{0:T(1024)S(1)} copy-done((s32[4096]{0:T(1024)S(1)}, s32[4096]{0:T(1024)}, u32[]{:S(2)}) %copy-start.4) | copy-done | bytes 16408
  7.6 12.6 %own_attention.1 = (bf16[128,6144]{1,0:T(8,128)(2,1)S(1)}, f32[128,128]{1,0:T(8,128)S(1)}, bf16[128,128]{1,0:T(8,128)(2,1)S(1)}) custom-call(bf16[128,6144]{1,0:T(8,128)(2,1)S(1)} %copy-done, bf16[128,1024]{1,0:T(8,128)(2,1)S(1)} %copy-done.1, bf16[128,1024]{1,0:T(8,128)(2,1)S(1)} %copy-done.2, s32[32,128]{1,0:T(8,128)S(1)} %bitcast.1), custom_call_target="tpu_custom_call" | custom-call | tf_op jit(solution)/shard_map/own_attention/pallas_call | solution.py:139
  20.2 0.0 copy-start.3
  20.2 0.0 collective-permute-done.1.key_near
  20.3 0.0 collective-permute-done.key_far
  20.3 3.6 %crossing_weights.1 = (bf16[48,128,128]{2,1,0:T(8,128)(2,1)S(1)}, f32[48,128,128]{2,1,0:T(8,128)S(1)}) custom-call(bf16[128,6144]{1,0:T(8,128)(2,1)S(1)} %copy-done, bf16[128,1024]{1,0:T(8,128)(2,1)S(1)} %copy-done.1, bf16[128,1024]{1,0:T(8,128)(2,1)S(1)} %collective-permute-done.key_far, bf16[128,1024]{1,0:T(8,128)(2,1)S(1)} %collective-permute-done.1.key_near, ...), custom_call_target="tpu_custom_call" | custom-call | tf_op jit(solution)/shard_map/crossing_weights/pallas_call | solution.py:152
  23.9 0.0 collective-permute-done.2.value_far
  23.9 0.0 collective-permute-done.3.value_near
  23.9 0.0 copy-done.3
  24.0 1.5 %merge.1 = bf16[128,6144]{1,0:T(8,128)(2,1)} custom-call(bf16[48,128,128]{2,1,0:T(8,128)(2,1)S(1)} %get-tuple-element.12.weights, f32[48,128,128]{2,1,0:T(8,128)S(1)} %get-tuple-element.13.share, bf16[128,1024]{1,0:T(8,128)(2,1)S(1)} %copy-done.3, bf16[128,1024]{1,0:T(8,128)(2,1)S(1)} %collective-permute-done.2.value_far, ...), custom_call_target="tpu_custom_call" | custom-call | tf_op jit(solution)/shard_map/merge/pallas_call | solution.py:163
Async XLA Ops:
  0.0 20.2 %collective-permute-start.1 = (bf16[128,1024]{1,0:T(8,128)(2,1)}, bf16[128,1024]{1,0:T(8,128)(2,1)S(1)}, u32[]{:S(2)}, u32[]{:S(2)}) collective-permute-start(bf16[128,1024]{1,0:T(8,128)(2,1)} %key.1), channel_id=1, source_target_pairs={{0,1},{1,0},{2,3},{3,2},{4,5},{5,4},{6,7},{7,6},{8,9},{9,8},{10,11... | collective-permute-start | bytes 786440 | tf_op jit(solution)/shard_map/ppermute | solution.py:130
  0.5 19.8 %collective-permute-start = (bf16[128,1024]{1,0:T(8,128)(2,1)}, bf16[128,1024]{1,0:T(8,128)(2,1)S(1)}, u32[]{:S(2)}, u32[]{:S(2)}) collective-permute-start(bf16[128,1024]{1,0:T(8,128)(2,1)} %key.1), channel_id=1, source_target_pairs={{0,1},{1,2},{2,3},{3,4},{4,5},{5,6},{6,7},{7,8},{8,9},{9,10},{10,1... | collective-permute-start | bytes 786440 | tf_op jit(solution)/shard_map/ppermute | solution.py:131
  0.5 23.4 %collective-permute-start.2 = (bf16[128,1024]{1,0:T(8,128)(2,1)}, bf16[128,1024]{1,0:T(8,128)(2,1)S(1)}, u32[]{:S(2)}, u32[]{:S(2)}) collective-permute-start(bf16[128,1024]{1,0:T(8,128)(2,1)} %value.1), channel_id=1, source_target_pairs={{0,1},{1,2},{2,3},{3,4},{4,5},{5,6},{6,7},{7,8},{8,9},{9,10},{10,1... | collective-permute-start | bytes 786440 | tf_op jit(solution)/shard_map/ppermute | solution.py:133
  3.1 20.9 %collective-permute-start.3 = (bf16[128,1024]{1,0:T(8,128)(2,1)}, bf16[128,1024]{1,0:T(8,128)(2,1)S(1)}, u32[]{:S(2)}, u32[]{:S(2)}) collective-permute-start(bf16[128,1024]{1,0:T(8,128)(2,1)} %value.1), channel_id=1, source_target_pairs={{0,1},{1,0},{2,3},{3,2},{4,5},{5,4},{6,7},{7,6},{8,9},{9,8},{10,11... | collective-permute-start | bytes 786440 | tf_op jit(solution)/shard_map/ppermute | solution.py:132
  3.6 1.4 %copy-start = (bf16[128,6144]{1,0:T(8,128)(2,1)S(1)}, bf16[128,6144]{1,0:T(8,128)(2,1)}, u32[]{:S(2)}) copy-start(bf16[128,6144]{1,0:T(8,128)(2,1)} %query.1) | copy-start | bytes 4718596
  5.0 0.9 %copy-start.1 = (bf16[128,1024]{1,0:T(8,128)(2,1)S(1)}, bf16[128,1024]{1,0:T(8,128)(2,1)}, u32[]{:S(2)}) copy-start(bf16[128,1024]{1,0:T(8,128)(2,1)} %key.1) | copy-start | bytes 786436
  5.9 0.9 %copy-start.2 = (bf16[128,1024]{1,0:T(8,128)(2,1)S(1)}, bf16[128,1024]{1,0:T(8,128)(2,1)}, u32[]{:S(2)}) copy-start(bf16[128,1024]{1,0:T(8,128)(2,1)} %value.1) | copy-start | bytes 786436
  6.9 0.7 %copy-start.4 = (s32[4096]{0:T(1024)S(1)}, s32[4096]{0:T(1024)}, u32[]{:S(2)}) copy-start(s32[4096]{0:T(1024)} %param.7) | copy-start | bytes 49156
  20.2 3.7 %copy-start.3 = (bf16[128,1024]{1,0:T(8,128)(2,1)S(1)}, bf16[128,1024]{1,0:T(8,128)(2,1)}, u32[]{:S(2)}) copy-start(bf16[128,1024]{1,0:T(8,128)(2,1)} %value.1) | copy-start | bytes 786436

commit v2 on v1

v2 whole, which is shorter than its diff:
```python
import functools
import math

import jax
import jax.numpy as jnp
from jax import lax
from jax.experimental import pallas as pl
from jax.experimental.pallas import tpu as pltpu
from jax.sharding import PartitionSpec as P

HQ = 48
KV = 8
HEAD = 128
PER_KV = HQ // KV
TOKENS_AXES = ("ctx", "ulysses")
HIDDEN = -1e30
EXPONENT = math.log2(math.e) / math.sqrt(HEAD)
KERNEL_VMEM = 16 * 1024 * 1024


def two_rings(count, cut):
    first = [(i, i + 1) for i in range(cut)] + [(cut, 0)]
    second = [(i, i + 1) for i in range(cut + 1, count - 1)] + [(count - 1, cut + 1)]
    return first + second


def ring(count, steps):
    return [(i, (i + steps) % count) for i in range(count)]


def swapped(count):
    return [(i, i ^ 1) for i in range(count)]


def head_columns(head, heads=1):
    return slice(head * HEAD, (head + heads) * HEAD)


def column_softmax(raw):
    peak = jnp.max(raw, axis=0, keepdims=True)
    weights = jnp.exp2((raw - peak) * EXPONENT)
    return weights, 1.0 / jnp.sum(weights, axis=0, keepdims=True)


def raw_scores(keys, query, head, bias):
    raw = lax.dot_general(
        keys,
        jnp.concatenate([query[:, head_columns(head)], query[:, head_columns(head + 1)]], axis=0),
        (((1,), (1,)), ((), ())),
        preferred_element_type=jnp.float32,
    )
    return raw + jnp.concatenate([bias, bias], axis=1)


def own_kernel(
    query_in, key_in, value_in, docs_in, own, query, key, value, cross_bias, crossing, own_bias, docs, sems
):
    length = key.shape[0]
    width = PER_KV * HEAD
    pieces = [(docs_in, docs), (key_in, key)]
    pieces += [(query_in.at[:, g * width : (g + 1) * width], query.at[:, g * width : (g + 1) * width]) for g in range(KV)]
    pieces.insert(3, (value_in, value))
    copies = [pltpu.make_async_copy(source, target, sems.at[i]) for i, (source, target) in enumerate(pieces)]
    for copy in copies:
        copy.start()
    copies[0].wait()
    me = lax.axis_index(TOKENS_AXES)
    own_docs = docs[pl.ds(me, 1), :]
    before = jnp.where(me > 0, docs[pl.ds(jnp.maximum(me - 1, 0), 1), :], -1)
    row = lax.broadcasted_iota(jnp.int32, (length, length), 0)
    column = lax.broadcasted_iota(jnp.int32, (length, length), 1)
    diagonal = row == column
    key_doc = jnp.sum(jnp.where(diagonal, own_docs, 0), axis=1, keepdims=True)
    before_doc = jnp.sum(jnp.where(diagonal, before, 0), axis=1, keepdims=True)
    own_seen = (key_doc == own_docs) & (row <= column)
    own_bias[...] = jnp.where(own_seen, 0.0, HIDDEN)
    cross_bias[...] = jnp.where(own_seen | (before_doc == own_docs), 0.0, HIDDEN)
    crossing[...] = jnp.where(key_doc == before[:, length - 1 :], jnp.ones((length, length), jnp.float32), 0.0).astype(
        jnp.bfloat16
    )
    copies[1].wait()
    for g in range(KV):
        copies[2 if g == 0 else g + 3].wait()
        if g == 0:
            copies[3].wait()
        keys = key[:, head_columns(g)]
        values = value[:, head_columns(g)].T
        for head in range(g * PER_KV, (g + 1) * PER_KV, 2):
            weights, share = column_softmax(raw_scores(keys, query, head, own_bias[...]))
            mixed = jnp.dot(values, weights.astype(jnp.bfloat16), preferred_element_type=jnp.float32)
            mixed = (mixed * share).astype(jnp.bfloat16)
            own[:, head_columns(head)] = mixed[:, :length].T
            own[:, head_columns(head + 1)] = mixed[:, length:].T


def weight_kernel(query, key, key_far, key_near, cross_bias, crossing, weights_out, share_out, *, cut):
    length = key.shape[0]
    from_near = lax.axis_index(TOKENS_AXES) == cut + 1
    mine = crossing[...] > 0
    for g in range(KV):
        columns = head_columns(g)
        behind = jnp.where(from_near, key_near[:, columns], key_far[:, columns])
        keys = jnp.where(mine, key[:, columns], behind)
        for head in range(g * PER_KV, (g + 1) * PER_KV, 2):
            weights, share = column_softmax(raw_scores(keys, query, head, cross_bias[...]))
            weights = weights.astype(jnp.bfloat16)
            for i in range(2):
                part = slice(i * length, (i + 1) * length)
                weights_out[head + i] = weights[:, part].T
                share_out[head + i] = jnp.broadcast_to(share[:, part], (HEAD, length)).T


def merge_kernel(weights, share, value, value_far, value_near, crossing, own, out, held, sems, *, cut):
    from_near = lax.axis_index(TOKENS_AXES) == cut + 1
    mine = crossing[...] > 0
    copies = []
    for g in range(KV):
        columns = head_columns(g)
        behind = jnp.where(from_near, value_near[:, columns], value_far[:, columns])
        values = jnp.where(mine, value[:, columns], behind)
        for head in range(g * PER_KV, (g + 1) * PER_KV):
            mixed = jnp.dot(weights[head], values, preferred_element_type=jnp.float32)
            fresh = (mixed * share[head]).astype(jnp.bfloat16)
            held[:, head_columns(head)] = jnp.where(mine, fresh, own[:, head_columns(head)])
        group = head_columns(g * PER_KV, PER_KV)
        copies.append(pltpu.make_async_copy(held.at[:, group], out.at[:, group], sems.at[g]))
        copies[-1].start()
    for copy in copies:
        copy.wait()


def in_vmem(array):
    return pltpu.with_memory_space_constraint(array, pltpu.VMEM)


def one_block_back(queries, keys, values, doc_ids):
    count = lax.axis_size(TOKENS_AXES)
    length = queries.shape[0]
    cut = count // 2 - 2
    rings, swap = two_rings(count, cut), swapped(count)
    key_far = lax.ppermute(keys, TOKENS_AXES, rings)
    key_near = lax.ppermute(keys, TOKENS_AXES, swap)
    value_far = lax.ppermute(values, TOKENS_AXES, rings)
    value_near = lax.ppermute(values, TOKENS_AXES, swap)
    docs = doc_ids.reshape(-1, length)
    whole = pl.BlockSpec(memory_space=pltpu.VMEM)
    anywhere = pl.BlockSpec(memory_space=pl.ANY)
    params = pltpu.CompilerParams(vmem_limit_bytes=KERNEL_VMEM)
    square = (length, length)
    own, query_held, key_held, value_held, cross_bias, crossing = pl.pallas_call(
        own_kernel,
        out_shape=(
            pltpu.VMEM(queries.shape, jnp.bfloat16),
            pltpu.VMEM(queries.shape, jnp.bfloat16),
            pltpu.VMEM(keys.shape, jnp.bfloat16),
            pltpu.VMEM(values.shape, jnp.bfloat16),
            pltpu.VMEM(square, jnp.float32),
            pltpu.VMEM(square, jnp.bfloat16),
        ),
        in_specs=[pl.BlockSpec(memory_space=pltpu.HBM)] * 4,
        out_specs=[whole] * 6,
        scratch_shapes=[
            pltpu.VMEM(square, jnp.float32),
            pltpu.VMEM(docs.shape, jnp.int32),
            pltpu.SemaphoreType.DMA((KV + 3,)),
        ],
        compiler_params=params,
        name="own_attention",
    )(*(pltpu.with_memory_space_constraint(array, pltpu.HBM) for array in (queries, keys, values, docs)))
    weights, share = pl.pallas_call(
        functools.partial(weight_kernel, cut=cut),
        out_shape=(
            pltpu.VMEM((HQ,) + square, jnp.bfloat16),
            pltpu.VMEM((HQ,) + square, jnp.float32),
        ),
        in_specs=[whole] * 6,
        out_specs=[whole] * 2,
        compiler_params=params,
        name="crossing_weights",
    )(query_held, key_held, in_vmem(key_far), in_vmem(key_near), cross_bias, crossing)
    return pl.pallas_call(
        functools.partial(merge_kernel, cut=cut),
        out_shape=jax.ShapeDtypeStruct(queries.shape, jnp.bfloat16),
        in_specs=[whole] * 7,
        out_specs=anywhere,
        scratch_shapes=[pltpu.VMEM(queries.shape, jnp.bfloat16), pltpu.SemaphoreType.DMA((KV,))],
        compiler_params=params,
        name="merge",
    )(weights, share, value_held, in_vmem(value_far), in_vmem(value_near), crossing, own)


def blocks_back(queries, keys, values, doc_ids, blocks):
    count = lax.axis_size(TOKENS_AXES)
    length = queries.shape[0]
    me = lax.axis_index(TOKENS_AXES)
    halo = [
        (lax.ppermute(keys, TOKENS_AXES, ring(count, s)), lax.ppermute(values, TOKENS_AXES, ring(count, s)))
        for s in range(blocks, 0, -1)
    ] + [(keys, values)]
    window = (blocks + 1) * length
    key_all = jnp.concatenate([k for k, _ in halo], axis=0).reshape(window, KV, HEAD).transpose(1, 0, 2)
    value_all = jnp.concatenate([v for _, v in halo], axis=0).reshape(window, KV, HEAD).transpose(1, 0, 2)
    padded = jnp.concatenate([jnp.full((blocks * length,), -1, jnp.int32), doc_ids], axis=0)
    key_doc = lax.dynamic_slice_in_dim(padded, me * length, window, 0)
    query_doc = key_doc[blocks * length :]
    offset = jnp.arange(window, dtype=jnp.int32) - blocks * length
    visible = (key_doc[None, :] == query_doc[:, None]) & (offset[None, :] <= jnp.arange(length)[:, None])
    grouped = queries.reshape(length, KV, PER_KV, HEAD).transpose(1, 2, 0, 3)

    def one_head(operands):
        rows, key_rows, value_rows = operands
        raw = jnp.einsum("gqd,kd->gqk", rows, key_rows, preferred_element_type=jnp.float32)
        raw = jnp.where(visible[None], raw, HIDDEN)
        peak = jnp.max(raw, axis=-1, keepdims=True)
        weights = jnp.exp2((raw - peak) * EXPONENT)
        totals = jnp.sum(weights, axis=-1, keepdims=True)
        mixed = jnp.einsum("gqk,kd->gqd", weights.astype(jnp.bfloat16), value_rows, preferred_element_type=jnp.float32)
        return (mixed / totals).astype(jnp.bfloat16)

    mixed = lax.map(one_head, (grouped, key_all, value_all))
    return mixed.transpose(2, 0, 1, 3).reshape(length, HQ * HEAD)


def shards(queries, keys, values, doc_ids):
    length = queries.shape[0]
    reach = lax.axis_size("ulysses") * length // 4
    blocks = -(-reach // length)
    if blocks == 1 and length == HEAD:
        return one_block_back(queries, keys, values, doc_ids)
    return blocks_back(queries, keys, values, doc_ids, blocks)


def solution(mesh):
    placed = P(TOKENS_AXES, None)
    return jax.shard_map(
        shards, mesh=mesh, in_specs=(placed, placed, placed, P()), out_specs=placed, check_vma=False
    )
```

time: 25.7 us -> 14 us (0.54)
  Pallas kernels: 17.8 us -> 8.9 us
  local copies, waits for them, and re-layouts: 4.03 us -> 0 us
  starting transfers between devices: 3.56 us -> 4.66 us
    pallas_call x1, Pallas kernels: 12.6 us -> 5.47 us  [one_block_back(): pl.pallas_call(own_kernel, out_shape=(pltpu.VMEM(queries.shape, jnp.bfloa...]
    unnamed x10 -> x0, local copies, waits for them, and re-layouts: 4.03 us -> none
    ppermute x1, starting transfers between devices: 2.55 us -> 0.01 us  [one_block_back(): value_far = lax.ppermute(values, TOKENS_AXES, rings)]
    ppermute x1, starting transfers between devices: 0.45 us -> 2.6 us  [one_block_back(): key_near = lax.ppermute(keys, TOKENS_AXES, swap)]
    pallas_call x1, Pallas kernels: 3.65 us -> 1.95 us  [one_block_back(): pl.pallas_call(functools.partial(weight_kernel, cut=cut), out_shape=(pltp...]
    ppermute x1, starting transfers between devices: 0.51 us -> 1.6 us  [one_block_back(): value_near = lax.ppermute(values, TOKENS_AXES, swap)]
    ppermute x1, starting transfers between devices: 0.06 us -> 0.45 us  [one_block_back(): key_far = lax.ppermute(keys, TOKENS_AXES, rings)]
  transfers between devices with their start and end apart: 4 -> 4, of which waited for: 0 -> 1; matrix products, arithmetic and copies ran while one was open for 0% -> 0% of each run, Pallas kernels for 64% -> 54%
where the time goes in v2:
time: 14 us; the launch traced here: 13.8 us
  Pallas kernels  8.9 us (64%)
  starting transfers between devices  4.66 us (33%)
  waiting for transfers between devices  0.17 us (1%)
    pallas_call x1, Pallas kernels, one_block_back(): pl.pallas_call(own_kernel, out_shape=(pltpu.VMEM(queries.shape, jnp.bfloa...  5.47 us
    ppermute x1, starting transfers between devices, one_block_back(): key_near = lax.ppermute(keys, TOKENS_AXES, swap)  2.6 us
    pallas_call x1, Pallas kernels, one_block_back(): pl.pallas_call(functools.partial(weight_kernel, cut=cut), out_shape=(pltp...  1.95 us
    ppermute x1, starting transfers between devices, one_block_back(): value_near = lax.ppermute(values, TOKENS_AXES, swap)  1.6 us
    pallas_call x1, Pallas kernels, one_block_back(): pl.pallas_call(functools.partial(merge_kernel, cut=cut), out_shape=jax.Sh...  1.48 us
    ppermute x1, starting transfers between devices, one_block_back(): key_far = lax.ppermute(keys, TOKENS_AXES, rings)  0.45 us
  transfers between devices with their start and end apart: 4, of which 1 were waited for; matrix products, arithmetic and copies ran while one was open for 0% of the time, Pallas kernels for 54%

profile of v2, /device:TPU:0, one launch (start us, length us, event | category | flops | bytes accessed | tf_op | source)
XLA Modules:
  0.0 13.8 jit_solution(3104645269255489467)
XLA Ops:
  0.0 0.5 %collective-permute-start = (bf16[128,1024]{1,0:T(8,128)(2,1)}, bf16[128,1024]{1,0:T(8,128)(2,1)S(1)}, u32[]{:S(2)}, u32[]{:S(2)}) collective-permute-start(bf16[128,1024]{1,0:T(8,128)(2,1)} %key_in.1), channel_id=1, source_target_pairs={{0,1},{1,2},{2,3},{3,4},{4,5},{5,6},{6,7},{7,8},{8,9},{9,10},{10,1... | collective-permute-start | bytes 786440 | tf_op jit(solution)/shard_map/ppermute | solution.py:141
  0.5 2.6 %collective-permute-start.1 = (bf16[128,1024]{1,0:T(8,128)(2,1)}, bf16[128,1024]{1,0:T(8,128)(2,1)S(1)}, u32[]{:S(2)}, u32[]{:S(2)}) collective-permute-start(bf16[128,1024]{1,0:T(8,128)(2,1)} %key_in.1), channel_id=1, source_target_pairs={{0,1},{1,0},{2,3},{3,2},{4,5},{5,4},{6,7},{7,6},{8,9},{9,8},{10,11... | collective-permute-start | bytes 786440 | tf_op jit(solution)/shard_map/ppermute | solution.py:142
  3.1 0.0 collective-permute-start.2
  3.1 1.6 %collective-permute-start.3 = (bf16[128,1024]{1,0:T(8,128)(2,1)}, bf16[128,1024]{1,0:T(8,128)(2,1)S(1)}, u32[]{:S(2)}, u32[]{:S(2)}) collective-permute-start(bf16[128,1024]{1,0:T(8,128)(2,1)} %value_in.1), channel_id=1, source_target_pairs={{0,1},{1,0},{2,3},{3,2},{4,5},{5,4},{6,7},{7,6},{8,9},{9,8},{10,11... | collective-permute-start | bytes 786440 | tf_op jit(solution)/shard_map/ppermute | solution.py:144
  4.7 5.5 %own_attention.1 = (bf16[128,6144]{1,0:T(8,128)(2,1)S(1)}, bf16[128,6144]{1,0:T(8,128)(2,1)S(1)}, bf16[128,1024]{1,0:T(8,128)(2,1)S(1)}, bf16[128,1024]{1,0:T(8,...) custom-call(bf16[128,6144]{1,0:T(8,128)(2,1)} %query_in.1, bf16[128,1024]{1,0:T(8,128)(2,1)} %key_in.1, ...), custom_call_target="tpu_custom_call" | custom-call | tf_op jit(solution)/shard_map/own_attention/pallas_call | solution.py:150
  10.1 0.0 collective-permute-done.key_far
  10.1 0.0 collective-permute-done.1.key_near
  10.2 1.9 %crossing_weights.1 = (bf16[48,128,128]{2,1,0:T(8,128)(2,1)S(1)}, f32[48,128,128]{2,1,0:T(8,128)S(1)}) custom-call(bf16[128,6144]{1,0:T(8,128)(2,1)S(1)} %get-tuple-element.13.query, bf16[128,1024]{1,0:T(8,128)(2,1)S(1)} %get-tuple-element.14.key, bf16[128,1024]{1,0:T(8,128)(2,1)S(1)} %collective-permute-done.key_far, ...), custom_call_target="tpu_custom_call" | custom-call | tf_op jit(solution)/shard_map/crossing_weights/pallas_call | solution.py:170
  12.1 0.2 %collective-permute-done.2.value_far = bf16[128,1024]{1,0:T(8,128)(2,1)S(1)} collective-permute-done((bf16[128,1024]{1,0:T(8,128)(2,1)}, bf16[128,1024]{1,0:T(8,128)(2,1)S(1)}, u32[]{:S(2)}, u32[]{:S(2)}) %collective-permute-start.2) | collective-permute-done | bytes 262176 | tf_op jit(solution)/shard_map/ppermute | solution.py:143
  12.3 0.0 collective-permute-done.3.value_near
  12.3 1.5 %merge.1 = bf16[128,6144]{1,0:T(8,128)(2,1)} custom-call(bf16[48,128,128]{2,1,0:T(8,128)(2,1)S(1)} %get-tuple-element.17.weights, f32[48,128,128]{2,1,0:T(8,128)S(1)} %get-tuple-element.18.share, bf16[128,1024]{1,0:T(8,128)(2,1)S(1)} %get-tuple-element.19.value, bf16[128,1024]{1,0:T(8,128)(2,1)S(1)} %collective-permute-done.2.value_far, ...), custom_call_target="tpu_custom_call" | custom-call | tf_op jit(solution)/shard_map/merge/pallas_call | solution.py:181
Async XLA Ops:
  0.0 10.1 %collective-permute-start = (bf16[128,1024]{1,0:T(8,128)(2,1)}, bf16[128,1024]{1,0:T(8,128)(2,1)S(1)}, u32[]{:S(2)}, u32[]{:S(2)}) collective-permute-start(bf16[128,1024]{1,0:T(8,128)(2,1)} %key_in.1), channel_id=1, source_target_pairs={{0,1},{1,2},{2,3},{3,4},{4,5},{5,6},{6,7},{7,8},{8,9},{9,10},{10,1... | collective-permute-start | bytes 786440 | tf_op jit(solution)/shard_map/ppermute | solution.py:141
  0.5 9.7 %collective-permute-start.1 = (bf16[128,1024]{1,0:T(8,128)(2,1)}, bf16[128,1024]{1,0:T(8,128)(2,1)S(1)}, u32[]{:S(2)}, u32[]{:S(2)}) collective-permute-start(bf16[128,1024]{1,0:T(8,128)(2,1)} %key_in.1), channel_id=1, source_target_pairs={{0,1},{1,0},{2,3},{3,2},{4,5},{5,4},{6,7},{7,6},{8,9},{9,8},{10,11... | collective-permute-start | bytes 786440 | tf_op jit(solution)/shard_map/ppermute | solution.py:142
  3.1 9.2 %collective-permute-start.2 = (bf16[128,1024]{1,0:T(8,128)(2,1)}, bf16[128,1024]{1,0:T(8,128)(2,1)S(1)}, u32[]{:S(2)}, u32[]{:S(2)}) collective-permute-start(bf16[128,1024]{1,0:T(8,128)(2,1)} %value_in.1), channel_id=1, source_target_pairs={{0,1},{1,2},{2,3},{3,4},{4,5},{5,6},{6,7},{7,8},{8,9},{9,10},{10,1... | collective-permute-start | bytes 786440 | tf_op jit(solution)/shard_map/ppermute | solution.py:143
  3.1 9.2 %collective-permute-start.3 = (bf16[128,1024]{1,0:T(8,128)(2,1)}, bf16[128,1024]{1,0:T(8,128)(2,1)S(1)}, u32[]{:S(2)}, u32[]{:S(2)}) collective-permute-start(bf16[128,1024]{1,0:T(8,128)(2,1)} %value_in.1), channel_id=1, source_target_pairs={{0,1},{1,0},{2,3},{3,2},{4,5},{5,4},{6,7},{7,6},{8,9},{9,8},{10,11... | collective-permute-start | bytes 786440 | tf_op jit(solution)/shard_map/ppermute | solution.py:144

commit v3 on v2

--- a/solution.py
+++ b/solution.py
@@ -57,9 +57,8 @@
 ):
     length = key.shape[0]
     width = PER_KV * HEAD
-    pieces = [(docs_in, docs), (key_in, key)]
+    pieces = [(docs_in, docs), (key_in, key), (value_in, value)]
     pieces += [(query_in.at[:, g * width : (g + 1) * width], query.at[:, g * width : (g + 1) * width]) for g in range(KV)]
-    pieces.insert(3, (value_in, value))
     copies = [pltpu.make_async_copy(source, target, sems.at[i]) for i, (source, target) in enumerate(pieces)]
     for copy in copies:
         copy.start()
@@ -78,11 +77,9 @@
     crossing[...] = jnp.where(key_doc == before[:, length - 1 :], jnp.ones((length, length), jnp.float32), 0.0).astype(
         jnp.bfloat16
     )
-    copies[1].wait()
+    for copy in copies[1:]:
+        copy.wait()
     for g in range(KV):
-        copies[2 if g == 0 else g + 3].wait()
-        if g == 0:
-            copies[3].wait()
         keys = key[:, head_columns(g)]
         values = value[:, head_columns(g)].T
         for head in range(g * PER_KV, (g + 1) * PER_KV, 2):
@@ -138,10 +135,10 @@
     length = queries.shape[0]
     cut = count // 2 - 2
     rings, swap = two_rings(count, cut), swapped(count)
+    key_near = lax.ppermute(keys, TOKENS_AXES, swap)
+    value_near = lax.ppermute(values, TOKENS_AXES, swap)
     key_far = lax.ppermute(keys, TOKENS_AXES, rings)
-    key_near = lax.ppermute(keys, TOKENS_AXES, swap)
     value_far = lax.ppermute(values, TOKENS_AXES, rings)
-    value_near = lax.ppermute(values, TOKENS_AXES, swap)
     docs = doc_ids.reshape(-1, length)
     whole = pl.BlockSpec(memory_space=pltpu.VMEM)
     anywhere = pl.BlockSpec(memory_space=pl.ANY)

time: 14 us -> 14 us (level)
  waiting for transfers between devices: 0.17 us -> 2.39 us
  Pallas kernels: 8.9 us -> 6.69 us
    pallas_call x1, Pallas kernels: 5.47 us -> 3.26 us  [one_block_back(): pl.pallas_call(own_kernel, out_shape=(pltpu.VMEM(queries.shape, jnp.bfloa...]
    ppermute x1, waiting for transfers between devices: 0.01 us -> 1.53 us  [one_block_back(): key_far = lax.ppermute(keys, TOKENS_AXES, rings)]
    ppermute x1, waiting for transfers between devices: 0.16 us -> 0.85 us  [one_block_back(): value_far = lax.ppermute(values, TOKENS_AXES, rings)]
  transfers between devices with their start and end apart: 4 -> 4, of which waited for: 1 -> 2; matrix products, arithmetic and copies ran while one was open for 0% -> 0% of each run, Pallas kernels for 54% -> 38%
where the time goes in v3:
time: 14 us; the launch traced here: 13.8 us
  Pallas kernels  6.69 us (48%)
  starting transfers between devices  4.66 us (33%)
  waiting for transfers between devices  2.39 us (17%)
    pallas_call x1, Pallas kernels, one_block_back(): pl.pallas_call(own_kernel, out_shape=(pltpu.VMEM(queries.shape, jnp.bfloa...  3.26 us
    ppermute x1, starting transfers between devices, one_block_back(): key_near = lax.ppermute(keys, TOKENS_AXES, swap)  2.6 us
    pallas_call x1, Pallas kernels, one_block_back(): pl.pallas_call(functools.partial(weight_kernel, cut=cut), out_shape=(pltp...  1.95 us
    ppermute x1, starting transfers between devices, one_block_back(): value_near = lax.ppermute(values, TOKENS_AXES, swap)  1.6 us
    ppermute x1, waiting for transfers between devices, one_block_back(): key_far = lax.ppermute(keys, TOKENS_AXES, rings)  1.53 us
    pallas_call x1, Pallas kernels, one_block_back(): pl.pallas_call(functools.partial(merge_kernel, cut=cut), out_shape=jax.Sh...  1.48 us
    ppermute x1, waiting for transfers between devices, one_block_back(): value_far = lax.ppermute(values, TOKENS_AXES, rings)  0.85 us
    ppermute x1, starting transfers between devices, one_block_back(): key_far = lax.ppermute(keys, TOKENS_AXES, rings)  0.45 us
  transfers between devices with their start and end apart: 4, of which 2 were waited for; matrix products, arithmetic and copies ran while one was open for 0% of the time, Pallas kernels for 38%

profile of v3, /device:TPU:0, one launch (start us, length us, event | category | flops | bytes accessed | tf_op | source)
XLA Modules:
  0.0 13.8 jit_solution(417859150603674441)
XLA Ops:
  0.0 0.5 %collective-permute-start = (bf16[128,1024]{1,0:T(8,128)(2,1)}, bf16[128,1024]{1,0:T(8,128)(2,1)S(1)}, u32[]{:S(2)}, u32[]{:S(2)}) collective-permute-start(bf16[128,1024]{1,0:T(8,128)(2,1)} %key_in.1), channel_id=1, source_target_pairs={{0,1},{1,2},{2,3},{3,4},{4,5},{5,6},{6,7},{7,8},{8,9},{9,10},{10,1... | collective-permute-start | bytes 786440 | tf_op jit(solution)/shard_map/ppermute | solution.py:140
  0.5 2.6 %collective-permute-start.1 = (bf16[128,1024]{1,0:T(8,128)(2,1)}, bf16[128,1024]{1,0:T(8,128)(2,1)S(1)}, u32[]{:S(2)}, u32[]{:S(2)}) collective-permute-start(bf16[128,1024]{1,0:T(8,128)(2,1)} %key_in.1), channel_id=1, source_target_pairs={{0,1},{1,0},{2,3},{3,2},{4,5},{5,4},{6,7},{7,6},{8,9},{9,8},{10,11... | collective-permute-start | bytes 786440 | tf_op jit(solution)/shard_map/ppermute | solution.py:138
  3.1 0.0 collective-permute-start.2
  3.1 1.6 %collective-permute-start.3 = (bf16[128,1024]{1,0:T(8,128)(2,1)}, bf16[128,1024]{1,0:T(8,128)(2,1)S(1)}, u32[]{:S(2)}, u32[]{:S(2)}) collective-permute-start(bf16[128,1024]{1,0:T(8,128)(2,1)} %value_in.1), channel_id=1, source_target_pairs={{0,1},{1,0},{2,3},{3,2},{4,5},{5,4},{6,7},{7,6},{8,9},{9,8},{10,11... | collective-permute-start | bytes 786440 | tf_op jit(solution)/shard_map/ppermute | solution.py:139
  4.7 3.3 %own_attention.1 = (bf16[128,6144]{1,0:T(8,128)(2,1)S(1)}, bf16[128,6144]{1,0:T(8,128)(2,1)S(1)}, bf16[128,1024]{1,0:T(8,128)(2,1)S(1)}, bf16[128,1024]{1,0:T(8,...) custom-call(bf16[128,6144]{1,0:T(8,128)(2,1)} %query_in.1, bf16[128,1024]{1,0:T(8,128)(2,1)} %key_in.1, ...), custom_call_target="tpu_custom_call" | custom-call | tf_op jit(solution)/shard_map/own_attention/pallas_call | solution.py:147
  7.9 1.5 %collective-permute-done.key_far = bf16[128,1024]{1,0:T(8,128)(2,1)S(1)} collective-permute-done((bf16[128,1024]{1,0:T(8,128)(2,1)}, bf16[128,1024]{1,0:T(8,128)(2,1)S(1)}, u32[]{:S(2)}, u32[]{:S(2)}) %collective-permute-start) | collective-permute-done | bytes 262176 | tf_op jit(solution)/shard_map/ppermute | solution.py:140
  9.5 0.0 collective-permute-done.1.key_near
  9.5 1.9 %crossing_weights.1 = (bf16[48,128,128]{2,1,0:T(8,128)(2,1)S(1)}, f32[48,128,128]{2,1,0:T(8,128)S(1)}) custom-call(bf16[128,6144]{1,0:T(8,128)(2,1)S(1)} %get-tuple-element.13.query, bf16[128,1024]{1,0:T(8,128)(2,1)S(1)} %get-tuple-element.14.key, bf16[128,1024]{1,0:T(8,128)(2,1)S(1)} %collective-permute-done.key_far, ...), custom_call_target="tpu_custom_call" | custom-call | tf_op jit(solution)/shard_map/crossing_weights/pallas_call | solution.py:167
  11.4 0.9 %collective-permute-done.2.value_far = bf16[128,1024]{1,0:T(8,128)(2,1)S(1)} collective-permute-done((bf16[128,1024]{1,0:T(8,128)(2,1)}, bf16[128,1024]{1,0:T(8,128)(2,1)S(1)}, u32[]{:S(2)}, u32[]{:S(2)}) %collective-permute-start.2) | collective-permute-done | bytes 262176 | tf_op jit(solution)/shard_map/ppermute | solution.py:141
  12.3 0.0 collective-permute-done.3.value_near
  12.3 1.5 %merge.1 = bf16[128,6144]{1,0:T(8,128)(2,1)} custom-call(bf16[48,128,128]{2,1,0:T(8,128)(2,1)S(1)} %get-tuple-element.17.weights, f32[48,128,128]{2,1,0:T(8,128)S(1)} %get-tuple-element.18.share, bf16[128,1024]{1,0:T(8,128)(2,1)S(1)} %get-tuple-element.19.value, bf16[128,1024]{1,0:T(8,128)(2,1)S(1)} %collective-permute-done.2.value_far, ...), custom_call_target="tpu_custom_call" | custom-call | tf_op jit(solution)/shard_map/merge/pallas_call | solution.py:178
Async XLA Ops:
  0.0 9.5 %collective-permute-start = (bf16[128,1024]{1,0:T(8,128)(2,1)}, bf16[128,1024]{1,0:T(8,128)(2,1)S(1)}, u32[]{:S(2)}, u32[]{:S(2)}) collective-permute-start(bf16[128,1024]{1,0:T(8,128)(2,1)} %key_in.1), channel_id=1, source_target_pairs={{0,1},{1,2},{2,3},{3,4},{4,5},{5,6},{6,7},{7,8},{8,9},{9,10},{10,1... | collective-permute-start | bytes 786440 | tf_op jit(solution)/shard_map/ppermute | solution.py:140
  0.5 9.0 %collective-permute-start.1 = (bf16[128,1024]{1,0:T(8,128)(2,1)}, bf16[128,1024]{1,0:T(8,128)(2,1)S(1)}, u32[]{:S(2)}, u32[]{:S(2)}) collective-permute-start(bf16[128,1024]{1,0:T(8,128)(2,1)} %key_in.1), channel_id=1, source_target_pairs={{0,1},{1,0},{2,3},{3,2},{4,5},{5,4},{6,7},{7,6},{8,9},{9,8},{10,11... | collective-permute-start | bytes 786440 | tf_op jit(solution)/shard_map/ppermute | solution.py:138
  3.1 9.2 %collective-permute-start.2 = (bf16[128,1024]{1,0:T(8,128)(2,1)}, bf16[128,1024]{1,0:T(8,128)(2,1)S(1)}, u32[]{:S(2)}, u32[]{:S(2)}) collective-permute-start(bf16[128,1024]{1,0:T(8,128)(2,1)} %value_in.1), channel_id=1, source_target_pairs={{0,1},{1,2},{2,3},{3,4},{4,5},{5,6},{6,7},{7,8},{8,9},{9,10},{10,1... | collective-permute-start | bytes 786440 | tf_op jit(solution)/shard_map/ppermute | solution.py:141
  3.1 9.2 %collective-permute-start.3 = (bf16[128,1024]{1,0:T(8,128)(2,1)}, bf16[128,1024]{1,0:T(8,128)(2,1)S(1)}, u32[]{:S(2)}, u32[]{:S(2)}) collective-permute-start(bf16[128,1024]{1,0:T(8,128)(2,1)} %value_in.1), channel_id=1, source_target_pairs={{0,1},{1,0},{2,3},{3,2},{4,5},{5,4},{6,7},{7,6},{8,9},{9,8},{10,11... | collective-permute-start | bytes 786440 | tf_op jit(solution)/shard_map/ppermute | solution.py:139

commit v4 on v3

--- a/solution.py
+++ b/solution.py
@@ -18,10 +18,21 @@
 KERNEL_VMEM = 16 * 1024 * 1024
 
 
-def two_rings(count, cut):
-    first = [(i, i + 1) for i in range(cut)] + [(cut, 0)]
-    second = [(i, i + 1) for i in range(cut + 1, count - 1)] + [(count - 1, cut + 1)]
-    return first + second
+def cuts_of(count):
+    return [cut for cut in [4, 6] + list(range(14, count, 8)) if cut < count - 2]
+
+
+def rings_between(count, cuts):
+    pairs, first = [], 0
+    for last in cuts + [count - 1]:
+        pairs += [(i, i + 1) for i in range(first, last)] + [(last, first)]
+        first = last + 1
+    return pairs
+
+
+def after_cut(cuts):
+    me = lax.axis_index(TOKENS_AXES)
+    return functools.reduce(jnp.logical_or, [me == cut + 1 for cut in cuts], False)
 
 
 def ring(count, steps):
@@ -90,9 +101,9 @@
             own[:, head_columns(head + 1)] = mixed[:, length:].T
 
 
-def weight_kernel(query, key, key_far, key_near, cross_bias, crossing, weights_out, share_out, *, cut):
+def weight_kernel(query, key, key_near, key_far, cross_bias, crossing, weights_out, share_out, *, cuts):
     length = key.shape[0]
-    from_near = lax.axis_index(TOKENS_AXES) == cut + 1
+    from_near = after_cut(cuts)
     mine = crossing[...] > 0
     for g in range(KV):
         columns = head_columns(g)
@@ -107,8 +118,8 @@
                 share_out[head + i] = jnp.broadcast_to(share[:, part], (HEAD, length)).T
 
 
-def merge_kernel(weights, share, value, value_far, value_near, crossing, own, out, held, sems, *, cut):
-    from_near = lax.axis_index(TOKENS_AXES) == cut + 1
+def merge_kernel(weights, share, value, value_far, value_near, crossing, own, out, held, sems, *, cuts):
+    from_near = after_cut(cuts)
     mine = crossing[...] > 0
     copies = []
     for g in range(KV):
@@ -133,11 +144,11 @@
 def one_block_back(queries, keys, values, doc_ids):
     count = lax.axis_size(TOKENS_AXES)
     length = queries.shape[0]
-    cut = count // 2 - 2
-    rings, swap = two_rings(count, cut), swapped(count)
+    cuts = cuts_of(count)
+    rings, swap = rings_between(count, cuts), swapped(count)
     key_near = lax.ppermute(keys, TOKENS_AXES, swap)
+    key_far = lax.ppermute(keys, TOKENS_AXES, rings)
     value_near = lax.ppermute(values, TOKENS_AXES, swap)
-    key_far = lax.ppermute(keys, TOKENS_AXES, rings)
     value_far = lax.ppermute(values, TOKENS_AXES, rings)
     docs = doc_ids.reshape(-1, length)
     whole = pl.BlockSpec(memory_space=pltpu.VMEM)
@@ -165,7 +176,7 @@
         name="own_attention",
     )(*(pltpu.with_memory_space_constraint(array, pltpu.HBM) for array in (queries, keys, values, docs)))
     weights, share = pl.pallas_call(
-        functools.partial(weight_kernel, cut=cut),
+        functools.partial(weight_kernel, cuts=cuts),
         out_shape=(
             pltpu.VMEM((HQ,) + square, jnp.bfloat16),
             pltpu.VMEM((HQ,) + square, jnp.float32),
@@ -174,9 +185,9 @@
         out_specs=[whole] * 2,
         compiler_params=params,
         name="crossing_weights",
-    )(query_held, key_held, in_vmem(key_far), in_vmem(key_near), cross_bias, crossing)
+    )(query_held, key_held, in_vmem(key_near), in_vmem(key_far), cross_bias, crossing)
     return pl.pallas_call(
-        functools.partial(merge_kernel, cut=cut),
+        functools.partial(merge_kernel, cuts=cuts),
         out_shape=jax.ShapeDtypeStruct(queries.shape, jnp.bfloat16),
         in_specs=[whole] * 7,
         out_specs=anywhere,

time: 14 us -> 12.3 us (0.88)
  the two profiles are of different devices: /device:TPU:0 before, /device:TPU:16 now
where the time goes in v4:
time: 12.3 us; the launch traced here: 12.1 us
  Pallas kernels  6.68 us (54%)
  waiting for transfers between devices  3.27 us (27%)
  starting transfers between devices  2.12 us (17%)
    pallas_call x1, Pallas kernels, one_block_back(): pl.pallas_call(own_kernel, out_shape=(pltpu.VMEM(queries.shape, jnp.bfloa...  3.26 us
    ppermute x1, waiting for transfers between devices, one_block_back(): key_far = lax.ppermute(keys, TOKENS_AXES, rings)  2.41 us
    pallas_call x1, Pallas kernels, one_block_back(): pl.pallas_call(functools.partial(weight_kernel, cuts=cuts), out_shape=(pl...  1.94 us
    pallas_call x1, Pallas kernels, one_block_back(): pl.pallas_call(functools.partial(merge_kernel, cuts=cuts), out_shape=jax....  1.47 us
    ppermute x1, starting transfers between devices, one_block_back(): value_far = lax.ppermute(values, TOKENS_AXES, rings)  1.1 us
    ppermute x1, waiting for transfers between devices, one_block_back(): value_far = lax.ppermute(values, TOKENS_AXES, rings)  0.86 us
    ppermute x1, starting transfers between devices, one_block_back(): value_near = lax.ppermute(values, TOKENS_AXES, swap)  0.51 us
    ppermute x1, starting transfers between devices, one_block_back(): key_far = lax.ppermute(keys, TOKENS_AXES, rings)  0.51 us
  transfers between devices with their start and end apart: 4, of which 2 were waited for; matrix products, arithmetic and copies ran while one was open for 0% of the time, Pallas kernels for 43%

profile of v4, /device:TPU:16, one launch (start us, length us, event | category | flops | bytes accessed | tf_op | source)
XLA Modules:
  0.0 12.1 jit_solution(4978458500820573267)
XLA Ops:
  0.0 0.0 collective-permute-start
  0.0 0.5 %collective-permute-start.1 = (bf16[128,1024]{1,0:T(8,128)(2,1)}, bf16[128,1024]{1,0:T(8,128)(2,1)S(1)}, u32[]{:S(2)}, u32[]{:S(2)}) collective-permute-start(bf16[128,1024]{1,0:T(8,128)(2,1)} %key_in.1), channel_id=1, source_target_pairs={{0,1},{1,2},{2,3},{3,4},{4,0},{5,6},{6,5},{7,8},{8,9},{9,10},{10,1... | collective-permute-start | bytes 786440 | tf_op jit(solution)/shard_map/ppermute | solution.py:150
  0.5 1.1 %collective-permute-start.2 = (bf16[128,1024]{1,0:T(8,128)(2,1)}, bf16[128,1024]{1,0:T(8,128)(2,1)S(1)}, u32[]{:S(2)}, u32[]{:S(2)}) collective-permute-start(bf16[128,1024]{1,0:T(8,128)(2,1)} %value_in.1), channel_id=1, source_target_pairs={{0,1},{1,2},{2,3},{3,4},{4,0},{5,6},{6,5},{7,8},{8,9},{9,10},{10,1... | collective-permute-start | bytes 786440 | tf_op jit(solution)/shard_map/ppermute | solution.py:152
  1.6 0.5 %collective-permute-start.3 = (bf16[128,1024]{1,0:T(8,128)(2,1)}, bf16[128,1024]{1,0:T(8,128)(2,1)S(1)}, u32[]{:S(2)}, u32[]{:S(2)}) collective-permute-start(bf16[128,1024]{1,0:T(8,128)(2,1)} %value_in.1), channel_id=1, source_target_pairs={{0,1},{1,0},{2,3},{3,2},{4,5},{5,4},{6,7},{7,6},{8,9},{9,8},{10,11... | collective-permute-start | bytes 786440 | tf_op jit(solution)/shard_map/ppermute | solution.py:151
  2.1 3.3 %own_attention.1 = (bf16[128,6144]{1,0:T(8,128)(2,1)S(1)}, bf16[128,6144]{1,0:T(8,128)(2,1)S(1)}, bf16[128,1024]{1,0:T(8,128)(2,1)S(1)}, bf16[128,1024]{1,0:T(8,...) custom-call(bf16[128,6144]{1,0:T(8,128)(2,1)} %query_in.1, bf16[128,1024]{1,0:T(8,128)(2,1)} %key_in.1, ...), custom_call_target="tpu_custom_call" | custom-call | tf_op jit(solution)/shard_map/own_attention/pallas_call | solution.py:158
  5.4 0.0 collective-permute-done.key_near
  5.4 2.4 %collective-permute-done.1.key_far = bf16[128,1024]{1,0:T(8,128)(2,1)S(1)} collective-permute-done((bf16[128,1024]{1,0:T(8,128)(2,1)}, bf16[128,1024]{1,0:T(8,128)(2,1)S(1)}, u32[]{:S(2)}, u32[]{:S(2)}) %collective-permute-start.1) | collective-permute-done | bytes 262176 | tf_op jit(solution)/shard_map/ppermute | solution.py:150
  7.8 1.9 %crossing_weights.1 = (bf16[48,128,128]{2,1,0:T(8,128)(2,1)S(1)}, f32[48,128,128]{2,1,0:T(8,128)S(1)}) custom-call(bf16[128,6144]{1,0:T(8,128)(2,1)S(1)} %get-tuple-element.13.query, bf16[128,1024]{1,0:T(8,128)(2,1)S(1)} %get-tuple-element.14.key, bf16[128,1024]{1,0:T(8,128)(2,1)S(1)} %collective-permute-done.key_near, ...), custom_call_target="tpu_custom_call" | custom-call | tf_op jit(solution)/shard_map/crossing_weights/pallas_call | solution.py:178
  9.8 0.9 %collective-permute-done.2.value_far = bf16[128,1024]{1,0:T(8,128)(2,1)S(1)} collective-permute-done((bf16[128,1024]{1,0:T(8,128)(2,1)}, bf16[128,1024]{1,0:T(8,128)(2,1)S(1)}, u32[]{:S(2)}, u32[]{:S(2)}) %collective-permute-start.2) | collective-permute-done | bytes 262176 | tf_op jit(solution)/shard_map/ppermute | solution.py:152
  10.6 0.0 collective-permute-done.3.value_near
  10.6 1.5 %merge.1 = bf16[128,6144]{1,0:T(8,128)(2,1)} custom-call(bf16[48,128,128]{2,1,0:T(8,128)(2,1)S(1)} %get-tuple-element.17.weights, f32[48,128,128]{2,1,0:T(8,128)S(1)} %get-tuple-element.18.share, bf16[128,1024]{1,0:T(8,128)(2,1)S(1)} %get-tuple-element.19.value, bf16[128,1024]{1,0:T(8,128)(2,1)S(1)} %collective-permute-done.2.value_far, ...), custom_call_target="tpu_custom_call" | custom-call | tf_op jit(solution)/shard_map/merge/pallas_call | solution.py:189
Async XLA Ops:
  0.0 5.4 %collective-permute-start = (bf16[128,1024]{1,0:T(8,128)(2,1)}, bf16[128,1024]{1,0:T(8,128)(2,1)S(1)}, u32[]{:S(2)}, u32[]{:S(2)}) collective-permute-start(bf16[128,1024]{1,0:T(8,128)(2,1)} %key_in.1), channel_id=1, source_target_pairs={{0,1},{1,0},{2,3},{3,2},{4,5},{5,4},{6,7},{7,6},{8,9},{9,8},{10,11... | collective-permute-start | bytes 786440 | tf_op jit(solution)/shard_map/ppermute | solution.py:149
  0.0 7.8 %collective-permute-start.1 = (bf16[128,1024]{1,0:T(8,128)(2,1)}, bf16[128,1024]{1,0:T(8,128)(2,1)S(1)}, u32[]{:S(2)}, u32[]{:S(2)}) collective-permute-start(bf16[128,1024]{1,0:T(8,128)(2,1)} %key_in.1), channel_id=1, source_target_pairs={{0,1},{1,2},{2,3},{3,4},{4,0},{5,6},{6,5},{7,8},{8,9},{9,10},{10,1... | collective-permute-start | bytes 786440 | tf_op jit(solution)/shard_map/ppermute | solution.py:150
  0.5 10.1 %collective-permute-start.2 = (bf16[128,1024]{1,0:T(8,128)(2,1)}, bf16[128,1024]{1,0:T(8,128)(2,1)S(1)}, u32[]{:S(2)}, u32[]{:S(2)}) collective-permute-start(bf16[128,1024]{1,0:T(8,128)(2,1)} %value_in.1), channel_id=1, source_target_pairs={{0,1},{1,2},{2,3},{3,4},{4,0},{5,6},{6,5},{7,8},{8,9},{9,10},{10,1... | collective-permute-start | bytes 786440 | tf_op jit(solution)/shard_map/ppermute | solution.py:152
  1.6 9.0 %collective-permute-start.3 = (bf16[128,1024]{1,0:T(8,128)(2,1)}, bf16[128,1024]{1,0:T(8,128)(2,1)S(1)}, u32[]{:S(2)}, u32[]{:S(2)}) collective-permute-start(bf16[128,1024]{1,0:T(8,128)(2,1)} %value_in.1), channel_id=1, source_target_pairs={{0,1},{1,0},{2,3},{3,2},{4,5},{5,4},{6,7},{7,6},{8,9},{9,8},{10,11... | collective-permute-start | bytes 786440 | tf_op jit(solution)/shard_map/ppermute | solution.py:151

commit v5 on v4

--- a/solution.py
+++ b/solution.py
@@ -64,16 +64,31 @@
 
 
 def own_kernel(
-    query_in, key_in, value_in, docs_in, own, query, key, value, cross_bias, crossing, own_bias, docs, sems
+    query_in,
+    key_in,
+    value_in,
+    docs_in,
+    own,
+    query,
+    key,
+    value,
+    cross_bias,
+    crossing,
+    own_bias,
+    docs,
+    docs_sem,
+    key_sem,
+    value_sem,
+    query_sem,
 ):
     length = key.shape[0]
-    width = PER_KV * HEAD
-    pieces = [(docs_in, docs), (key_in, key), (value_in, value)]
-    pieces += [(query_in.at[:, g * width : (g + 1) * width], query.at[:, g * width : (g + 1) * width]) for g in range(KV)]
-    copies = [pltpu.make_async_copy(source, target, sems.at[i]) for i, (source, target) in enumerate(pieces)]
+    docs_copy = pltpu.make_async_copy(docs_in, docs, docs_sem)
+    pieces = [(key_in, key, key_sem), (value_in, value, value_sem), (query_in, query, query_sem)]
+    copies = [pltpu.make_async_copy(source, target, sem) for source, target, sem in pieces]
+    docs_copy.start()
     for copy in copies:
         copy.start()
-    copies[0].wait()
+    docs_copy.wait()
     me = lax.axis_index(TOKENS_AXES)
     own_docs = docs[pl.ds(me, 1), :]
     before = jnp.where(me > 0, docs[pl.ds(jnp.maximum(me - 1, 0), 1), :], -1)
@@ -88,7 +103,7 @@
     crossing[...] = jnp.where(key_doc == before[:, length - 1 :], jnp.ones((length, length), jnp.float32), 0.0).astype(
         jnp.bfloat16
     )
-    for copy in copies[1:]:
+    for copy in copies:
         copy.wait()
     for g in range(KV):
         keys = key[:, head_columns(g)]
@@ -118,10 +133,9 @@
                 share_out[head + i] = jnp.broadcast_to(share[:, part], (HEAD, length)).T
 
 
-def merge_kernel(weights, share, value, value_far, value_near, crossing, own, out, held, sems, *, cuts):
+def merge_kernel(weights, share, value, value_far, value_near, crossing, own, out, held, sem, *, cuts):
     from_near = after_cut(cuts)
     mine = crossing[...] > 0
-    copies = []
     for g in range(KV):
         columns = head_columns(g)
         behind = jnp.where(from_near, value_near[:, columns], value_far[:, columns])
@@ -131,10 +145,8 @@
             fresh = (mixed * share[head]).astype(jnp.bfloat16)
             held[:, head_columns(head)] = jnp.where(mine, fresh, own[:, head_columns(head)])
         group = head_columns(g * PER_KV, PER_KV)
-        copies.append(pltpu.make_async_copy(held.at[:, group], out.at[:, group], sems.at[g]))
-        copies[-1].start()
-    for copy in copies:
-        copy.wait()
+        pltpu.make_async_copy(held.at[:, group], out.at[:, group], sem).start()
+    pltpu.make_async_copy(held, out, sem).wait()
 
 
 def in_vmem(array):
@@ -170,7 +182,7 @@
         scratch_shapes=[
             pltpu.VMEM(square, jnp.float32),
             pltpu.VMEM(docs.shape, jnp.int32),
-            pltpu.SemaphoreType.DMA((KV + 3,)),
+            *[pltpu.SemaphoreType.DMA] * 4,
         ],
         compiler_params=params,
         name="own_attention",
@@ -191,7 +203,7 @@
         out_shape=jax.ShapeDtypeStruct(queries.shape, jnp.bfloat16),
         in_specs=[whole] * 7,
         out_specs=anywhere,
-        scratch_shapes=[pltpu.VMEM(queries.shape, jnp.bfloat16), pltpu.SemaphoreType.DMA((KV,))],
+        scratch_shapes=[pltpu.VMEM(queries.shape, jnp.bfloat16), pltpu.SemaphoreType.DMA],
         compiler_params=params,
         name="merge",
     )(weights, share, value_held, in_vmem(value_far), in_vmem(value_near), crossing, own)

time: 12.3 us -> 12.3 us (level)
  no operation moved by 1% of the time
where the time goes in v5:
time: 12.3 us; the launch traced here: 12 us
  Pallas kernels  6.63 us (54%)
  waiting for transfers between devices  3.26 us (27%)
  starting transfers between devices  2.12 us (17%)
    pallas_call x1, Pallas kernels, one_block_back(): pl.pallas_call(own_kernel, out_shape=(pltpu.VMEM(queries.shape, jnp.bfloa...  3.27 us
    ppermute x1, waiting for transfers between devices, one_block_back(): key_far = lax.ppermute(keys, TOKENS_AXES, rings)  2.4 us
    pallas_call x1, Pallas kernels, one_block_back(): pl.pallas_call(functools.partial(weight_kernel, cuts=cuts), out_shape=(pl...  1.94 us
    pallas_call x1, Pallas kernels, one_block_back(): pl.pallas_call(functools.partial(merge_kernel, cuts=cuts), out_shape=jax....  1.41 us
    ppermute x1, starting transfers between devices, one_block_back(): value_far = lax.ppermute(values, TOKENS_AXES, rings)  1.1 us
    ppermute x1, waiting for transfers between devices, one_block_back(): value_far = lax.ppermute(values, TOKENS_AXES, rings)  0.86 us
    ppermute x1, starting transfers between devices, one_block_back(): value_near = lax.ppermute(values, TOKENS_AXES, swap)  0.51 us
    ppermute x1, starting transfers between devices, one_block_back(): key_far = lax.ppermute(keys, TOKENS_AXES, rings)  0.51 us
  transfers between devices with their start and end apart: 4, of which 2 were waited for; matrix products, arithmetic and copies ran while one was open for 0% of the time, Pallas kernels for 43%

profile of v5, /device:TPU:16, one launch (start us, length us, event | category | flops | bytes accessed | tf_op | source)
XLA Modules:
  0.0 12.0 jit_solution(13008737926359367865)
XLA Ops:
  0.0 0.0 collective-permute-start
  0.0 0.5 %collective-permute-start.1 = (bf16[128,1024]{1,0:T(8,128)(2,1)}, bf16[128,1024]{1,0:T(8,128)(2,1)S(1)}, u32[]{:S(2)}, u32[]{:S(2)}) collective-permute-start(bf16[128,1024]{1,0:T(8,128)(2,1)} %key_in.1), channel_id=1, source_target_pairs={{0,1},{1,2},{2,3},{3,4},{4,0},{5,6},{6,5},{7,8},{8,9},{9,10},{10,1... | collective-permute-start | bytes 786440 | tf_op jit(solution)/shard_map/ppermute | solution.py:162
  0.5 1.1 %collective-permute-start.2 = (bf16[128,1024]{1,0:T(8,128)(2,1)}, bf16[128,1024]{1,0:T(8,128)(2,1)S(1)}, u32[]{:S(2)}, u32[]{:S(2)}) collective-permute-start(bf16[128,1024]{1,0:T(8,128)(2,1)} %value_in.1), channel_id=1, source_target_pairs={{0,1},{1,2},{2,3},{3,4},{4,0},{5,6},{6,5},{7,8},{8,9},{9,10},{10,1... | collective-permute-start | bytes 786440 | tf_op jit(solution)/shard_map/ppermute | solution.py:164
  1.6 0.5 %collective-permute-start.3 = (bf16[128,1024]{1,0:T(8,128)(2,1)}, bf16[128,1024]{1,0:T(8,128)(2,1)S(1)}, u32[]{:S(2)}, u32[]{:S(2)}) collective-permute-start(bf16[128,1024]{1,0:T(8,128)(2,1)} %value_in.1), channel_id=1, source_target_pairs={{0,1},{1,0},{2,3},{3,2},{4,5},{5,4},{6,7},{7,6},{8,9},{9,8},{10,11... | collective-permute-start | bytes 786440 | tf_op jit(solution)/shard_map/ppermute | solution.py:163
  2.1 3.3 %own_attention.1 = (bf16[128,6144]{1,0:T(8,128)(2,1)S(1)}, bf16[128,6144]{1,0:T(8,128)(2,1)S(1)}, bf16[128,1024]{1,0:T(8,128)(2,1)S(1)}, bf16[128,1024]{1,0:T(8,...) custom-call(bf16[128,6144]{1,0:T(8,128)(2,1)} %query_in.1, bf16[128,1024]{1,0:T(8,128)(2,1)} %key_in.1, ...), custom_call_target="tpu_custom_call" | custom-call | tf_op jit(solution)/shard_map/own_attention/pallas_call | solution.py:170
  5.4 0.0 collective-permute-done.key_near
  5.4 2.4 %collective-permute-done.1.key_far = bf16[128,1024]{1,0:T(8,128)(2,1)S(1)} collective-permute-done((bf16[128,1024]{1,0:T(8,128)(2,1)}, bf16[128,1024]{1,0:T(8,128)(2,1)S(1)}, u32[]{:S(2)}, u32[]{:S(2)}) %collective-permute-start.1) | collective-permute-done | bytes 262176 | tf_op jit(solution)/shard_map/ppermute | solution.py:162
  7.8 1.9 %crossing_weights.1 = (bf16[48,128,128]{2,1,0:T(8,128)(2,1)S(1)}, f32[48,128,128]{2,1,0:T(8,128)S(1)}) custom-call(bf16[128,6144]{1,0:T(8,128)(2,1)S(1)} %get-tuple-element.13.query, bf16[128,1024]{1,0:T(8,128)(2,1)S(1)} %get-tuple-element.14.key, bf16[128,1024]{1,0:T(8,128)(2,1)S(1)} %collective-permute-done.key_near, ...), custom_call_target="tpu_custom_call" | custom-call | tf_op jit(solution)/shard_map/crossing_weights/pallas_call | solution.py:190
  9.8 0.9 %collective-permute-done.2.value_far = bf16[128,1024]{1,0:T(8,128)(2,1)S(1)} collective-permute-done((bf16[128,1024]{1,0:T(8,128)(2,1)}, bf16[128,1024]{1,0:T(8,128)(2,1)S(1)}, u32[]{:S(2)}, u32[]{:S(2)}) %collective-permute-start.2) | collective-permute-done | bytes 262176 | tf_op jit(solution)/shard_map/ppermute | solution.py:164
  10.6 0.0 collective-permute-done.3.value_near
  10.6 1.4 %merge.1 = bf16[128,6144]{1,0:T(8,128)(2,1)} custom-call(bf16[48,128,128]{2,1,0:T(8,128)(2,1)S(1)} %get-tuple-element.17.weights, f32[48,128,128]{2,1,0:T(8,128)S(1)} %get-tuple-element.18.share, bf16[128,1024]{1,0:T(8,128)(2,1)S(1)} %get-tuple-element.19.value, bf16[128,1024]{1,0:T(8,128)(2,1)S(1)} %collective-permute-done.2.value_far, ...), custom_call_target="tpu_custom_call" | custom-call | tf_op jit(solution)/shard_map/merge/pallas_call | solution.py:201
Async XLA Ops:
  0.0 5.4 %collective-permute-start = (bf16[128,1024]{1,0:T(8,128)(2,1)}, bf16[128,1024]{1,0:T(8,128)(2,1)S(1)}, u32[]{:S(2)}, u32[]{:S(2)}) collective-permute-start(bf16[128,1024]{1,0:T(8,128)(2,1)} %key_in.1), channel_id=1, source_target_pairs={{0,1},{1,0},{2,3},{3,2},{4,5},{5,4},{6,7},{7,6},{8,9},{9,8},{10,11... | collective-permute-start | bytes 786440 | tf_op jit(solution)/shard_map/ppermute | solution.py:161
  0.0 7.8 %collective-permute-start.1 = (bf16[128,1024]{1,0:T(8,128)(2,1)}, bf16[128,1024]{1,0:T(8,128)(2,1)S(1)}, u32[]{:S(2)}, u32[]{:S(2)}) collective-permute-start(bf16[128,1024]{1,0:T(8,128)(2,1)} %key_in.1), channel_id=1, source_target_pairs={{0,1},{1,2},{2,3},{3,4},{4,0},{5,6},{6,5},{7,8},{8,9},{9,10},{10,1... | collective-permute-start | bytes 786440 | tf_op jit(solution)/shard_map/ppermute | solution.py:162
  0.5 10.1 %collective-permute-start.2 = (bf16[128,1024]{1,0:T(8,128)(2,1)}, bf16[128,1024]{1,0:T(8,128)(2,1)S(1)}, u32[]{:S(2)}, u32[]{:S(2)}) collective-permute-start(bf16[128,1024]{1,0:T(8,128)(2,1)} %value_in.1), channel_id=1, source_target_pairs={{0,1},{1,2},{2,3},{3,4},{4,0},{5,6},{6,5},{7,8},{8,9},{9,10},{10,1... | collective-permute-start | bytes 786440 | tf_op jit(solution)/shard_map/ppermute | solution.py:164
  1.6 9.0 %collective-permute-start.3 = (bf16[128,1024]{1,0:T(8,128)(2,1)}, bf16[128,1024]{1,0:T(8,128)(2,1)S(1)}, u32[]{:S(2)}, u32[]{:S(2)}) collective-permute-start(bf16[128,1024]{1,0:T(8,128)(2,1)} %value_in.1), channel_id=1, source_target_pairs={{0,1},{1,0},{2,3},{3,2},{4,5},{5,4},{6,7},{7,6},{8,9},{9,8},{10,11... | collective-permute-start | bytes 786440 | tf_op jit(solution)/shard_map/ppermute | solution.py:163
